TPU v7x, 512 devices: a whole 4x8x8 slice. The times are simulated.
512 devices in a mesh: dp: 16 (over y_lo, x), seq: 32 (over z, y_hi, core).
Axes of the slice: x: 4, y: 8 (y_hi: 2, y_lo: 4; y = y_hi * 4 + y_lo), z: 8, core: 2. Of those that a mesh axis runs over, the one named last changes fastest.
Arguments:
- gated_input: bfloat16 [16, 16384, 1024], P('dp', 'seq'), may hold values from -6 to 6
- cotangent: bfloat16 [16, 16384, 1024], P('dp', 'seq'), may hold values from -6 to 6
- lengths: int32 [16, 8], P('dp'), may hold values from 1 to 8192, 16384 in all within a row
- kernel: float32 [9, 1024], replicated, may hold values from -2 to 2
- norm_gain: float32 [1024], replicated, may hold values from 0.5 to 1.5
- out_weight: bfloat16 [1024, 1024], P('seq'), may hold values from -0.1875 to 0.1875
Outputs:
- grad_gated: bfloat16 [16, 16384, 1024], P('dp', 'seq')
- grad_weight: float32 [1024, 1024], P('seq')
- grad_kernel: float32 [9, 1024], replicated
- grad_gain: float32 [1024], replicated
Inputs may be any that keep to these rules, and one draw needn't show every extreme that they name: Each row holds the lengths of 8 utterances that fill the stream's 16384 frames exactly; in every row the longest is 8192.
All inputs are finite; a program needn't handle non-finite values.
Results may differ from a plain program's by a relative error of at most 0.0029.
Values may be sent and summed in bfloat16 or wider, within the bound.
A program may use at most 64 MiB of HBM per device.

v0:
```python
import jax
import jax.numpy as jnp
from jax import lax
from jax.sharding import PartitionSpec as P


def extended(block, sides, width):
    for axis, dim in sides:
        count = lax.axis_size(axis)
        forward = [(i, i + 1) for i in range(count - 1)]
        backward = [(target, source) for source, target in forward]
        low = lax.ppermute(
            lax.slice_in_dim(block, block.shape[dim] - width, None, axis=dim), axis, forward
        )
        high = lax.ppermute(lax.slice_in_dim(block, 0, width, axis=dim), axis, backward)
        block = jnp.concatenate([low, block, high], axis=dim)
    return block


def utter_ids(frame_pos, lengths_row):
    bounds = jnp.cumsum(lengths_row)
    return jnp.sum((frame_pos[:, None] >= bounds[None, :]).astype(jnp.int32), axis=1)


def normalize(conv_out, norm_gain):
    centre = conv_out - jnp.mean(conv_out, axis=1, keepdims=True)
    inverse = lax.rsqrt(jnp.mean(centre * centre, axis=1, keepdims=True) + 1e-05)
    normed = centre * inverse
    return (normed, inverse, normed * norm_gain)


def back_norm(back_act, scaled, normed, inverse, norm_gain):
    logistic = jax.nn.sigmoid(scaled)
    back_scaled = back_act * (logistic * (1.0 + scaled * (1.0 - logistic)))
    hidden = back_scaled * norm_gain
    back_conv = inverse * (
        hidden
        - jnp.mean(hidden, axis=1, keepdims=True)
        - normed * jnp.mean(hidden * normed, axis=1, keepdims=True)
    )
    return (back_scaled, back_conv)


def tap_sum(kernel, values, ids_src, ids_dst, offset, row_count, flip):
    tap_count = kernel.shape[0]
    running = jnp.zeros((row_count, values.shape[1]), jnp.float32)
    for tap_index in range(tap_count):
        lead_row = offset + (tap_count - 1 - tap_index if flip else tap_index)
        inside = (ids_src[lead_row : lead_row + row_count] == ids_dst).astype(jnp.float32)[:, None]
        running = running + kernel[tap_index] * values[lead_row : lead_row + row_count] * inside
    return running


def tap_products(tap_count, grads, values, ids_src, ids_dst, offset, row_count):
    collected = []
    for tap_index in range(tap_count):
        lead_row = offset + tap_index
        inside = (ids_src[lead_row : lead_row + row_count] == ids_dst).astype(jnp.float32)[:, None]
        collected.append(jnp.sum(grads * values[lead_row : lead_row + row_count] * inside, axis=0))
    return jnp.stack(collected)


def body(gated_input, cotangent, lengths, kernel, norm_gain, out_weight):
    frames = gated_input.shape[1]
    tap_count = kernel.shape[0]
    reach = tap_count // 2
    source = gated_input[0]
    upstream = cotangent[0]
    anchor = lax.axis_index("seq") * frames
    frame_pos = anchor - reach + jnp.arange(frames + 2 * reach, dtype=jnp.int32)
    ids_wide = utter_ids(frame_pos, lengths[0])
    ids_own = ids_wide[reach : reach + frames]
    widened = extended(source, (("seq", 0),), reach).astype(jnp.float32)
    conv_out = tap_sum(kernel, widened, ids_wide, ids_own, 0, frames, False)
    normed, inverse, scaled = normalize(conv_out, norm_gain)
    act = (scaled * jax.nn.sigmoid(scaled)).astype(jnp.bfloat16)
    back_act = lax.dot_general(
        upstream,
        lax.all_gather(out_weight, "seq", axis=0, tiled=True),
        (((1,), (1,)), ((), ())),
        preferred_element_type=jnp.float32,
    )
    back_scaled, back_conv = back_norm(back_act, scaled, normed, inverse, norm_gain)
    back_wide = extended(back_conv, (("seq", 0),), reach)
    grad_rows = tap_sum(kernel, back_wide, ids_wide, ids_own, 0, frames, True)
    kernel_terms = tap_products(tap_count, back_conv, widened, ids_wide, ids_own, 0, frames)
    gain_terms = jnp.sum(back_scaled * normed, axis=0)
    partial_value = lax.psum_scatter(
        lax.dot_general(
            act, upstream, (((0,), (0,)), ((), ())), preferred_element_type=jnp.float32
        ),
        "seq",
        scatter_dimension=0,
        tiled=True,
    )
    grad_weight = lax.psum(partial_value, "dp")
    grad_kernel, grad_gain = lax.psum((kernel_terms, gain_terms), ("dp", "seq"))
    return (grad_rows.astype(jnp.bfloat16)[None], grad_weight, grad_kernel, grad_gain)


def solution(mesh):
    return jax.shard_map(
        body,
        mesh=mesh,
        in_specs=(
            P("dp", "seq", None),
            P("dp", "seq", None),
            P("dp", None),
            P(),
            P(),
            P("seq", None),
        ),
        out_specs=(P("dp", "seq", None), P("seq", None), P(), P()),
        check_vma=False,
    )
```

profile of v0, /device:TPU:6, one launch (start us, length us, event | category | flops | bytes accessed | tf_op | source)
XLA Modules:
  0.0 425.2 jit_solution(17413616293866410946)
XLA Ops:
  7.2 0.0 copy-start
  7.2 0.0 all-gather.2.cloned.1.call-start
  7.2 0.7 all-gather.2.cloned.1.call-update
  7.9 0.0 reduce-scatter.2.cloned.1.call-start
  8.0 0.7 slice_bitcast_fusion.1
  8.7 1.7 collective-permute-start
  10.5 1.3 collective-permute-start.1
  11.8 0.8 reduce-window.8
  12.6 0.1 convert_reduce_fusion
  12.7 1.2 fusion.50
  13.9 0.1 fusion.45
  14.0 0.0 collective-permute-done
  14.0 5.2 %collective-permute-done.1 = bf16[4,1024]{1,0:T(4,128)(2,1)S(1)} collective-permute-done((bf16[4,1024]{1,0:T(4,128)(2,1)S(1)}, bf16[4,1024]{1,0:T(4,128)(2,1)S(1)}, u32[]{:S(2)}, u32[]{:S(2)}) %collective-permute-start.1) | collective-permute-done | bytes 8224 | tf_op jit(solution)/shard_map/ppermute | solution.py:15
  19.1 1.5 maximum_convert_fusion
  20.7 3.9 fusion.48
  24.6 0.0 copy-start.1
  24.6 0.0 copy-start.4
  24.6 0.3 multiply_reduce_fusion.11
  25.0 1.0 copy-done.1
  25.9 0.0 copy-done
  25.9 0.0 copy-done.4
  25.9 3.5 fusion.31
  29.4 0.0 reduce-scatter.2.cloned.1.call-update
  29.5 0.0 all-reduce.3.cloned.1.call-start
  29.5 76.9 %all-gather.2.cloned.1.call-done = bf16[1024,1024]{1,0:T(8,128)(2,1)} async-done(((bf16[32,1024]{1,0:T(8,128)(2,1)}), bf16[1024,1024]{1,0:T(8,128)(2,1)}) %all-gather.2.cloned.1.call-update) | async-done | bytes 2097168 | tf_op jit(solution)/shard_map/all_gather | solution.py:79
  106.4 0.0 copy-start.2
  106.4 4.6 %multiply_reduce_fusion = (f32[1024]{0:T(1024)S(1)}, f32[512]{0:T(512)S(1)}, f32[512]{0:T(512)S(1)}, f32[512,1024]{1,0:T(8,128)S(1)}) fusion(f32[512,1024]{1,0:T(8,128)} %copy-done.1, f32[512]{0:T(512)S(1)} %add_rsqrt_fusion, f32[512]{0:T(512)S(1)} %broadcast_multiply_fusion.2, f32[1024]{0:T(1024)S(1)} %copy-done.4, ...), kind=kOutput, calls=%fused_computation.41 | convolution fusion | flops 1082652672 | bytes 7356416 | tf_op jit(solution)/shard_map/dot_general | solution.py:77
  111.0 0.0 copy-done.2
  111.0 4.5 %multiply_reduce_fusion.1 = (f32[1024]{0:T(1024)S(1)}, f32[1024]{0:T(1024)S(1)}, f32[1024]{0:T(1024)S(1)}, f32[1024]{0:T(1024)S(1)}, f32[1024]{0:T(1024)S(1)}, /...) fusion(f32[520,1024]{1,0:T(8,128)S(1)} %maximum_convert_fusion, ...), kind=kLoop, calls=%fused_computation.42 | loop fusion | flops 17292288 | bytes 25231360 | tf_op jit(solution)/shard_map/reduce_sum | solution.py:59
  115.6 0.0 copy-start.3
  115.6 1.3 copy-done.3
  116.9 1.3 collective-permute-start.2
  118.2 3.0 collective-permute-start.3
  121.2 0.1 stack.39
  121.3 105.5 %all-reduce = (f32[9,1024]{1,0:T(8,128)}, f32[1024]{0:T(1024)}) all-reduce(f32[9,1024]{1,0:T(8,128)S(1)} %stack.39, f32[1024]{0:T(1024)S(1)} %get-tuple-element.13), channel_id=1, replica_groups=mesh['dp'=16,'seq'=32] {'dp','seq'}, use_global_device_ids=true, to_apply=%region_17.18 | all-reduce | flops 10240 | bytes 81920 | tf_op jit(solution)/shard_map/psum | solution.py:97
  226.8 31.5 %reduce-scatter.2.cloned.1.call-done = f32[32,1024]{1,0:T(8,128)} async-done(((f32[1024,1024]{1,0:T(8,128)}), f32[32,1024]{1,0:T(8,128)}) %reduce-scatter.2.cloned.1.call-update) | async-done | bytes 131088 | tf_op jit(solution)/shard_map/reduce_scatter | solution.py:88
  258.3 0.0 all-reduce.3.cloned.1.call-update
  258.4 0.0 collective-permute-done.2
  258.4 0.0 collective-permute-done.3
  258.4 13.4 %fusion.38 = bf16[1,512,1024]{2,1,0:T(8,128)(2,1)} fusion(f32[512]{0:T(512)S(1)} %get-tuple-element.41, f32[512,1024]{1,0:T(8,128)} %copy-done.3, f32[4,1024]{1,0:T(4,128)S(1)} %collective-permute-done.3, f32[1024]{0:T(1024)S(1)} %bitcast.51, f32[512]{0:T(512)S(1)} %get-tuple-element.39, f32[1024]{0:T(1024)S(1)} %bitcast.53, f32[512]{0:T(512)S(1)} %get-tuple-element.38, ...), kind=kLoop, calls=%fused_computation.68 | loop fusion | flops 17825792 | bytes 3231744 | tf_op jit(solution)/shard_map/broadcast_in_dim | solution.py:98
  271.7 145.4 %all-reduce.3.cloned.1.call-done = f32[32,1024]{1,0:T(8,128)} async-done(((f32[32,1024]{1,0:T(8,128)}), f32[32,1024]{1,0:T(8,128)}) %all-reduce.3.cloned.1.call-update) | async-done | bytes 131088 | tf_op jit(solution)/shard_map/psum | solution.py:96
  417.1 1.6 copy.11
  (5 shorter events, 0.0 us)
Async XLA Ops:
  7.2 18.8 %copy-start = (bf16[1,512,1024]{2,1,0:T(8,128)(2,1)S(1)}, bf16[1,512,1024]{2,1,0:T(8,128)(2,1)}, u32[]{:S(2)}) copy-start(bf16[1,512,1024]{2,1,0:T(8,128)(2,1)} %param.7) | copy-start | bytes 3145732
  7.2 99.2 %all-gather.2.cloned.1.call-start = ((), (), s32[]{:S(2)}) async-start(), calls=%async_computation.1 | async-start | bytes 2162688 | tf_op jit(solution)/shard_map/all_gather | solution.py:79
  7.9 250.4 %reduce-scatter.2.cloned.1.call-start = ((), (), s32[]{:S(2)}) async-start(), calls=%async_computation.2 | async-start | bytes 4325376 | tf_op jit(solution)/shard_map/reduce_scatter | solution.py:88
  8.7 5.2 %collective-permute-start = (bf16[4,1024]{1,0:T(4,128)(2,1)S(1)}, bf16[4,1024]{1,0:T(4,128)(2,1)S(1)}, u32[]{:S(2)}, u32[]{:S(2)}) collective-permute-start(bf16[4,1024]{1,0:T(4,128)(2,1)S(1)} %get-tuple-element.23), channel_id=1, source_target_pairs={{0,1},{1,2},{2,3},{3,4},{4,5},{5,6},{6,7},{7,8},{8,9},{9,10},{10,1... | collective-permute-start | bytes 24584 | tf_op jit(solution)/shard_map/ppermute | solution.py:12
  10.5 8.7 %collective-permute-start.1 = (bf16[4,1024]{1,0:T(4,128)(2,1)S(1)}, bf16[4,1024]{1,0:T(4,128)(2,1)S(1)}, u32[]{:S(2)}, u32[]{:S(2)}) collective-permute-start(bf16[4,1024]{1,0:T(4,128)(2,1)S(1)} %get-tuple-element.24), channel_id=1, source_target_pairs={{1,0},{2,1},{3,2},{4,3},{5,4},{6,5},{7,6},{8,7},{9,8},{10,9},{11,1... | collective-permute-start | bytes 24584 | tf_op jit(solution)/shard_map/ppermute | solution.py:15
  24.6 1.3 copy-start.1
  24.6 1.3 copy-start.4
  29.5 387.7 %all-reduce.3.cloned.1.call-start = ((), (), s32[]{:S(2)}) async-start(), calls=%async_computation.3 | async-start | bytes 262144 | tf_op jit(solution)/shard_map/psum | solution.py:96
  106.4 4.6 %copy-start.2 = (f32[512,1024]{1,0:T(8,128)S(1)}, f32[512,1024]{1,0:T(8,128)}, u32[]{:S(2)}) copy-start(f32[512,1024]{1,0:T(8,128)} %copy-done.1) | copy-start | bytes 6291460
  115.6 1.3 copy-start.3
  116.9 141.5 %collective-permute-start.2 = (f32[4,1024]{1,0:T(4,128)S(1)}, f32[4,1024]{1,0:T(4,128)S(1)}, u32[]{:S(2)}, u32[]{:S(2)}) collective-permute-start(f32[4,1024]{1,0:T(4,128)S(1)} %get-tuple-element.21), channel_id=1, source_target_pairs={{1,0},{2,1},{3,2},{4,3},{5,4},{6,5},{7,6},{8,7},{9,8},{10,9},{11,1... | collective-permute-start | bytes 49160 | tf_op jit(solution)/shard_map/ppermute | solution.py:15
  118.2 140.2 %collective-permute-start.3 = (f32[4,1024]{1,0:T(4,128)S(1)}, f32[4,1024]{1,0:T(4,128)S(1)}, u32[]{:S(2)}, u32[]{:S(2)}) collective-permute-start(f32[4,1024]{1,0:T(4,128)S(1)} %get-tuple-element.22), channel_id=1, source_target_pairs={{0,1},{1,2},{2,3},{3,4},{4,5},{5,6},{6,7},{7,8},{8,9},{9,10},{10,1... | collective-permute-start | bytes 49160 | tf_op jit(solution)/shard_map/ppermute | solution.py:12
Sparse Core Ops, SparseCore 0:
  11.4 94.9 all-gather.1
  111.2 147.0 reduce-scatter.1
  261.5 155.5 all-reduce.2
where the time goes:
time: 430 us; the launch traced here: 425 us
  waiting for transfers between devices  260 us (60%)
  blocking collectives  106 us (25%)
  other arithmetic  24.7 us (6%)
  between operations  13.9 us (3%)
  matrix products  8.07 us (2%)
  starting transfers between devices  7.47 us (2%)
  local copies, waits for them, and re-layouts  5.89 us (1%)
    psum x1, waiting for transfers between devices, body(): grad_weight = lax.psum(partial_value, 'dp')  145 us
    psum x1, blocking collectives, body(): grad_kernel, grad_gain = lax.psum((kernel_terms, gain_terms), ('dp', 'seq'))  106 us
    all_gather x1, waiting for transfers between devices, body(): lax.all_gather(out_weight, 'seq', axis=0, tiled=True)  76.9 us
    reduce_scatter x1, waiting for transfers between devices, body(): lax.psum_scatter(lax.dot_general(act, upstream, (((0,), (0,)), ((), ())),...  31.5 us
    broadcast_in_dim x1, other arithmetic, body(): grad_rows.astype(jnp.bfloat16)[None]  13.4 us
  transfers between devices with their start and end apart: 7, of which 4 were waited for; matrix products, arithmetic and copies ran while one was open for 8% of the time, Pallas kernels for 0%

commit v1 on v0

v1 whole, which is shorter than its diff:
```python
import functools

import jax
import jax.numpy as jnp
from jax import lax
from jax.experimental import pallas as pl
from jax.experimental.pallas import tpu as pltpu
from jax.sharding import PartitionSpec as P

F32, BF16 = jnp.float32, jnp.bfloat16
MESH = pl.DeviceIdType.MESH
FRAMES, D, KW = 512, 1024, 9
ROWS = 32
LANES = [slice(128 * j, 128 * j + 128) for j in range(8)]


def add_up(terms):
    return functools.reduce(lambda a, b: a + b, terms)


def fold(value):
    return add_up([value[8 * q : 8 * q + 8] for q in range(value.shape[0] // 8)])


def device(x, y, z, c):
    return (lax.rem(y, 4) * 4 + x, z * 4 + lax.div(y, 4) * 2 + c)


def kernel(
    gated, cot_hbm, lengths, taps, gain, weight,
    out_rows, out_weight, out_kernel, out_gain,
    xb, cot, cot_far, halo, xw, ids, mask, kb, normed, sig, inv, act, act_far, wfull,
    back, bcw, tacc,
    ga, gd, sa1, ra1, ra2, sa2, ra3, rd1, sd1, rd2, sd2, rd3, final, gathered,
    kp, rk1, rk2, kfull,
    local, sends, recvs,
):
    dp, seq = lax.axis_index("dp"), lax.axis_index("seq")
    yl, x = lax.div(dp, 4), lax.rem(dp, 4)
    z, yh, c = lax.div(seq, 4), lax.rem(lax.div(seq, 2), 2), lax.rem(seq, 2)
    y = yh * 4 + yl
    zy = z * 2 + yh
    flip = 1 - c
    other_core = (dp, seq + 1 - 2 * c)
    before = (dp, lax.rem(seq + 31, 32))
    after = (dp, lax.rem(seq + 1, 32))
    mine = lax.div(z, 4) == c

    barrier = pltpu.get_barrier_semaphore()

    def greet(target):
        pl.semaphore_signal(barrier, inc=1, device_id=target, device_id_type=MESH)

    def column(i):
        at = lax.rem(2 * z + c + i, 16)
        return at, device(x, y, lax.div(at, 2), lax.rem(at, 2))

    def row(i):
        at = lax.rem(2 * y + c + i, 16)
        return at, device(x, lax.div(at, 2), z, lax.rem(at, 2))

    def plane(i):
        at = lax.rem(x * 8 + z + i, 32)
        return device(lax.div(at, 8), y, lax.rem(at, 8), c)

    def slabs(i):
        at = lax.rem(zy + i, 16)
        return device(x, lax.rem(at, 2) * 4 + yl, lax.div(at, 2), c)

    def streams(i):
        at = lax.rem(dp + i, 16)
        return (at, seq)

    def across_x(i):
        at = lax.rem(x + i, 4)
        return at, device(at, y, z, c)

    def across_y(i):
        at = lax.rem(y + i, 8)
        return at, device(x, at, z, c)

    def loop(low, high, step):
        def one(i, none):
            step(i)
            return none

        lax.fori_loop(low, high, one, 0)

    loop(1, 16, lambda i: greet(column(i)[1]))
    loop(1, 16, lambda i: greet(row(i)[1]))
    loop(1, 32, lambda i: greet(plane(i)))
    loop(1, 16, lambda i: greet(slabs(i)))
    loop(1, 16, lambda i: greet(streams(i)))
    greet(before)
    greet(after)

    def copy(group, source, target_ref, target):
        return pltpu.make_async_remote_copy(
            src_ref=source, dst_ref=target_ref, send_sem=sends.at[group],
            recv_sem=recvs.at[group], device_id=target, device_id_type=MESH,
        )

    def send(group, source, target_ref, target):
        copy(group, source, target_ref, target).start()

    def arrived(group, ref):
        copy(group, ref, ref, other_core).wait_recv()

    def sent(group, ref):
        copy(group, ref, ref, other_core).wait_send()

    (HALO_A, HALO_B, W_THIN, W_WIDE, W_X, W_C1, W_C2, COT, ACT, RA1, RA2, RA3, RD1, RD2, RD3,
     GATHER, K1, K2, K3, BACK_A, BACK_B) = range(21)
    ACTS = 21

    get_x = pltpu.make_async_copy(gated.at[0], xb, local.at[0])
    thin = pl.ds(pl.multiple_of(128 * x, 128), 128)
    wide = pl.ds(512, 512)
    get_thin = pltpu.make_async_copy(weight.at[:, thin], wfull.at[zy, c, :, thin], local.at[1])
    get_wide = pltpu.make_async_copy(weight.at[:, wide], wfull.at[zy, c, :, wide], local.at[3])
    get_cot = pltpu.make_async_copy(cot_hbm.at[0], cot, local.at[2])
    get_x.start()
    get_thin.start()
    get_wide.start()
    get_cot.start()

    start = seq * FRAMES
    pos = lax.broadcasted_iota(jnp.int32, (FRAMES + 16, 128), 0) + (start - 8)
    bound = jnp.int32(0)
    number = jnp.zeros((FRAMES + 16, 128), jnp.int32)
    for u in range(8):
        bound = bound + lengths[0, u]
        number = number + (pos >= bound).astype(jnp.int32)
    ids[...] = jnp.where(pos < 0, -1, number)
    for k in range(KW):
        kb[k] = jnp.broadcast_to(taps[k : k + 1, :], (8, D))
    kb[KW] = jnp.broadcast_to(gain[0:1, :], (8, D))

    def masks(i):
        r = pl.multiple_of(i * 32, 32)
        own = ids[pl.ds(r + 8, 32), :]
        for k in range(KW):
            mask[k, pl.ds(r, 32), :] = jnp.where(ids[pl.ds(r + 4 + k, 32), :] == own, 1.0, 0.0)

    loop(0, FRAMES // 32, masks)
    get_thin.wait()
    get_wide.wait()
    get_x.wait()
    pl.semaphore_wait(barrier, 15 + 15 + 31 + 15 + 15 + 2)

    send(HALO_A, xb.at[pl.ds(FRAMES - 16, 16)], halo.at[0], after)
    send(HALO_B, xb.at[pl.ds(0, 16)], halo.at[1], before)

    def send_thin(i):
        send(W_THIN, wfull.at[zy, c, :, thin], wfull.at[zy, c, :, thin], slabs(i))

    def send_wide(i):
        send(W_WIDE, wfull.at[zy, c, :, wide], wfull.at[zy, c, :, wide], slabs(i))

    loop(1, 16, send_thin)
    loop(1, 16, send_wide)
    get_cot.wait()
    send(COT, cot, cot_far, other_core)

    def widen(i):
        r = pl.multiple_of(i * 32, 32)
        value = xb[pl.ds(r, 32), :].astype(F32)
        for j in range(8):
            xw[j, pl.ds(r + 8, 32), :] = value[:, LANES[j]]

    loop(0, FRAMES // 32, widen)
    arrived(HALO_A, halo.at[0])
    arrived(HALO_B, halo.at[1])
    low, high = halo[0].astype(F32), halo[1].astype(F32)
    for j in range(8):
        xw[j, 0:8, :] = low[8:16, LANES[j]]
        xw[j, FRAMES + 8 : FRAMES + 16, :] = high[0:8, LANES[j]]

    def spread(value):
        return jnp.tile(value, (ROWS // 8, 1))

    def conv(source, r, mirrored):
        sums = []
        for j in range(8):
            terms = []
            for k in range(KW):
                lead = KW - 1 - k if mirrored else k
                terms.append(
                    spread(kb[k, :, LANES[j]])
                    * (source[j, pl.ds(r + 4 + lead, ROWS), :] * mask[lead, pl.ds(r, ROWS), :])
                )
            sums.append(add_up(terms))
        return sums

    def forward(i):
        r = pl.multiple_of(i * ROWS, ROWS)
        parts = conv(xw, r, False)
        mean = jnp.sum(add_up(parts), axis=1, keepdims=True) * (1.0 / D)
        parts = [v - mean for v in parts]
        square = jnp.sum(add_up([v * v for v in parts]), axis=1, keepdims=True) * (1.0 / D)
        scale = lax.rsqrt(square + 1e-05)
        inv[pl.ds(r, ROWS), :] = jnp.broadcast_to(scale, (ROWS, 128))
        for j in range(8):
            unit = parts[j] * scale
            normed[pl.ds(r, ROWS), LANES[j]] = unit
            scaled = unit * spread(kb[KW, :, LANES[j]])
            logistic = jax.nn.sigmoid(scaled)
            sig[pl.ds(r, ROWS), LANES[j]] = logistic
            act[j // 4, pl.ds(r, ROWS), LANES[j % 4]] = (scaled * logistic).astype(BF16)

    for q in range(4):
        loop(q * 4, q * 4 + 4, forward)
        block = pl.ds(128 * q, 128)
        send(ACTS + q, act.at[flip, block], act_far.at[block], other_core)
        if q == 2:
            arrived(W_THIN, wfull.at[pl.ds(0, 15), c, :, pl.ds(0, 128)])
            for i in (1, 3, 2):
                send(W_X, wfull.at[:, c, :, thin], wfull.at[:, c, :, thin], across_x(i)[1])

    arrived(COT, cot_far)
    for q in range(4):
        arrived(ACTS + q, act_far.at[pl.ds(128 * q, 128)])
    over_frames = (((0,), (0,)), ((), ()))
    for i in (1, 3, 2, 0):
        at, target = across_x(i)
        columns = pl.ds(pl.multiple_of(256 * at, 256), 256)
        value = lax.dot_general(
            act[c], cot[:, columns], over_frames, preferred_element_type=F32
        ) + lax.dot_general(
            act_far[...], cot_far[:, columns], over_frames, preferred_element_type=F32
        )
        gd[at] = value[:, 128:].astype(BF16).reshape(4, 2, 2, 32, 128)
        if i == 0:
            sa1[...] = value[:, :128].reshape(4, 2, 2, 4, 8, 128)
        else:
            ga[at] = value[:, :128].astype(BF16)
            send(RA1, ga.at[at], ra1.at[i - 1], target)

    def owner(t):
        zi, ci = lax.div(t, 2), lax.rem(t, 2)
        zt = 4 * c + zi
        return zi, ci, jnp.logical_and(zt == z, ci == c), device(x, y, zt, ci)

    def send_d1(t):
        zi, ci, here, target = owner(t)

        @pl.when(here)
        def _():
            rd1[z] = gd[:, zi, :, ci]

        @pl.when(jnp.logical_not(here))
        def _():
            send(RD1, gd.at[:, zi, :, ci], rd1.at[z], target)

    loop(0, 8, send_d1)

    arrived(W_WIDE, wfull.at[pl.ds(0, 15), c, :, wide])
    send(W_C1, wfull.at[:, c, :, wide], wfull.at[:, c, :, wide], other_core)
    arrived(W_X, wfull.at[pl.ds(0, 12), c, :, wide])
    send(W_C2, wfull.at[:, c, :, pl.ds(0, 512)], wfull.at[:, c, :, pl.ds(0, 512)], other_core)
    arrived(W_C1, wfull.at[:, flip, :, wide])
    arrived(W_C2, wfull.at[:, flip, :, pl.ds(0, 512)])

    def matmul(i):
        value = wfull[pl.ds(4 * i, 4)].reshape(256, D)
        back[:, pl.ds(pl.multiple_of(256 * i, 256), 256)] = lax.dot_general(
            cot[...], value, (((1,), (1,)), ((), ())), preferred_element_type=F32
        )

    loop(0, 4, matmul)

    def backward(i, sums):
        r = pl.multiple_of(i * ROWS, ROWS)
        totals, ones, twos = [], [], []
        for j in range(8):
            g = spread(kb[KW, :, LANES[j]])
            unit = normed[pl.ds(r, ROWS), LANES[j]]
            logistic = sig[pl.ds(r, ROWS), LANES[j]]
            scaled = unit * g
            value = back[pl.ds(r, ROWS), LANES[j]] * (logistic * (1.0 + scaled * (1.0 - logistic)))
            totals.append(sums[j] + fold(value * unit))
            hidden = value * g
            bcw[j, pl.ds(r + 8, ROWS), :] = hidden
            ones.append(hidden)
            twos.append(hidden * unit)
        first = jnp.sum(add_up(ones), axis=1, keepdims=True) * (1.0 / D)
        second = jnp.sum(add_up(twos), axis=1, keepdims=True) * (1.0 / D)
        scale = inv[pl.ds(r, ROWS), :]
        for j in range(8):
            unit = normed[pl.ds(r, ROWS), LANES[j]]
            bcw[j, pl.ds(r + 8, ROWS), :] = scale * (
                bcw[j, pl.ds(r + 8, ROWS), :] - first - unit * second
            )
        return tuple(totals)

    sums = lax.fori_loop(
        0, FRAMES // ROWS, backward, tuple(jnp.zeros((8, 128), F32) for _ in range(8))
    )
    send(BACK_A, bcw.at[:, pl.ds(FRAMES, 8)], bcw.at[:, pl.ds(0, 8)], after)
    send(BACK_B, bcw.at[:, pl.ds(8, 8)], bcw.at[:, pl.ds(FRAMES + 8, 8)], before)

    for k in range(KW):
        tacc[k] = jnp.zeros((8, D), F32)

    def products(i):
        r = pl.multiple_of(i * 64, 64)
        for k in range(KW):
            inside = mask[k, pl.ds(r, 64), :]
            for j in range(8):
                tacc[k, :, LANES[j]] += fold(
                    bcw[j, pl.ds(r + 8, 64), :] * (xw[j, pl.ds(r + 4 + k, 64), :] * inside)
                )

    loop(0, FRAMES // 64, products)
    for k in range(KW):
        line = jnp.sum(tacc[k], axis=0, keepdims=True)
        for j in range(8):
            kp[2 * j + k // 5, k % 5 : k % 5 + 1, :] = line[:, LANES[j]]
    for j in range(8):
        kp[2 * j + 1, 4:5, :] = jnp.sum(sums[j], axis=0, keepdims=True)

    def send_k1(i):
        at, target = row(i)
        send(K1, kp.at[at], rk1.at[i - 1], target)

    loop(1, 16, send_k1)

    arrived(RA1, ra1)
    total = sa1[...].reshape(FRAMES, 128)
    sa1[...] = (
        total + ra1[0].astype(F32) + ra1[1].astype(F32) + ra1[2].astype(F32)
    ).reshape(4, 2, 2, 4, 8, 128)

    def send_a2(i):
        at, target = across_y(i)
        send(RA2, sa1.at[:, lax.div(at, 4), :, lax.rem(at, 4)], ra2.at[i - 1], target)

    loop(1, 8, send_a2)

    def owned(group, ref):
        @pl.when(mine)
        def _():
            arrived(group, ref.at[pl.ds(0, 7)])

        @pl.when(jnp.logical_not(mine))
        def _():
            arrived(group, ref)

    owned(RD1, rd1)
    sd1[...] = add_up([rd1[i].astype(F32) for i in range(8)])
    for i in (1, 3, 2):
        at, target = across_x(i)
        send(RD2, sd1.at[at], rd2.at[i - 1], target)

    arrived(K1, rk1)
    me = x * 8 + z
    rk2[me] = add_up([kp[2 * y + c]] + [rk1[i] for i in range(15)])
    loop(1, 32, lambda i: send(K2, rk2.at[me], rk2.at[me], plane(i)))

    arrived(BACK_A, bcw.at[:, pl.ds(0, 8)])
    arrived(BACK_B, bcw.at[:, pl.ds(FRAMES + 8, 8)])

    def rows_out(i):
        r = pl.multiple_of(i * ROWS, ROWS)
        parts = conv(bcw, r, True)
        for j in range(8):
            out_rows[0, pl.ds(r, ROWS), LANES[j]] = parts[j].astype(BF16)

    loop(0, 8, rows_out)

    arrived(RA2, ra2)
    sa2[...] = add_up([sa1[:, yh, :, yl]] + [ra2[i] for i in range(7)])

    def send_a3(t):
        zi, ci, here, target = owner(t)

        @pl.when(here)
        def _():
            ra3[z] = sa2[zi, ci]

        @pl.when(jnp.logical_not(here))
        def _():
            send(RA3, sa2.at[zi, ci], ra3.at[z], target)

    loop(0, 8, send_a3)

    arrived(RD2, rd2)
    sd2[...] = add_up([sd1[x], rd2[0], rd2[1], rd2[2]]).reshape(2, 4, 8, 128)

    def send_d3(i):
        at, target = across_y(i)
        send(RD3, sd2.at[lax.div(at, 4), lax.rem(at, 4)], rd3.at[i - 1], target)

    loop(1, 8, send_d3)

    loop(8, 16, rows_out)

    arrived(K2, rk2.at[pl.ds(0, 31)])
    own = 2 * y + c
    kfull[own] = add_up([rk2[i] for i in range(32)])
    loop(1, 16, lambda i: send(K3, kfull.at[own], kfull.at[own], row(i)[1]))

    owned(RA3, ra3)
    final[:, 0:128] = add_up([ra3[i] for i in range(8)])
    arrived(RD3, rd3)
    final[:, 128:256] = add_up([sd2[yh, yl]] + [rd3[i] for i in range(7)])
    gathered[dp] = final[...]
    loop(1, 16, lambda i: send(GATHER, final, gathered.at[dp], streams(i)))

    arrived(K3, kfull.at[pl.ds(0, 15)])
    for j in range(8):
        out_kernel[0:5, LANES[j]] = kfull[2 * j]
        out_kernel[5:9, LANES[j]] = kfull[2 * j + 1, 0:4]
        out_gain[0:1, LANES[j]] = kfull[2 * j + 1, 4:5]
    arrived(GATHER, gathered.at[pl.ds(0, 15)])
    for a in range(4):
        for b in range(4):
            out_weight[8 * a : 8 * a + 8, 256 * b : 256 * b + 256] = gathered[4 * a + b]

    sent(HALO_A, halo.at[0])
    sent(HALO_B, halo.at[1])
    sent(W_THIN, wfull.at[pl.ds(0, 15), c, :, pl.ds(0, 128)])
    sent(W_WIDE, wfull.at[pl.ds(0, 15), c, :, wide])
    sent(W_X, wfull.at[pl.ds(0, 12), c, :, wide])
    sent(W_C1, wfull.at[:, c, :, wide])
    sent(W_C2, wfull.at[:, c, :, wide])
    sent(COT, cot)
    for q in range(4):
        sent(ACTS + q, act_far.at[pl.ds(128 * q, 128)])
    sent(RA1, ra1)
    sent(RA2, ra2)

    @pl.when(mine)
    def _():
        sent(RA3, ra3.at[pl.ds(0, 7)])
        sent(RD1, rd1.at[pl.ds(0, 7)])

    @pl.when(jnp.logical_not(mine))
    def _():
        sent(RA3, ra3)
        sent(RD1, rd1)

    sent(RD2, rd2)
    sent(RD3, rd3)
    sent(GATHER, gathered.at[pl.ds(0, 15)])
    sent(K1, rk1)
    sent(K2, rk2.at[pl.ds(0, 31)])
    sent(K3, kfull.at[pl.ds(0, 15)])
    sent(BACK_A, bcw.at[:, pl.ds(0, 8)])
    sent(BACK_B, bcw.at[:, pl.ds(0, 8)])


def body(gated, cotangent, lengths, taps, gain, weight):
    v = pltpu.VMEM
    vmem, hbm = pl.BlockSpec(memory_space=v), pl.BlockSpec(memory_space=pl.ANY)
    rows, dweight, dkernel, dgain = pl.pallas_call(
        kernel,
        out_shape=(
            jax.ShapeDtypeStruct((1, FRAMES, D), BF16),
            jax.ShapeDtypeStruct((32, D), F32),
            jax.ShapeDtypeStruct((KW, D), F32),
            jax.ShapeDtypeStruct((1, D), F32),
        ),
        in_specs=[hbm, hbm, pl.BlockSpec(memory_space=pltpu.SMEM), vmem, vmem, hbm],
        out_specs=(vmem, vmem, vmem, vmem),
        scratch_shapes=[
            v((FRAMES, D), BF16),
            v((FRAMES, D), BF16),
            v((FRAMES, D), BF16),
            v((2, 16, D), BF16),
            v((8, FRAMES + 16, 128), F32),
            v((FRAMES + 16, 128), jnp.int32),
            v((KW, FRAMES, 128), F32),
            v((KW + 1, 8, D), F32),
            v((FRAMES, D), F32),
            v((FRAMES, D), F32),
            v((FRAMES, 128), F32),
            v((2, FRAMES, 512), BF16),
            v((FRAMES, 512), BF16),
            v((16, 2, 32, D), BF16),
            v((FRAMES, D), F32),
            v((8, FRAMES + 16, 128), F32),
            v((KW, 8, D), F32),
            v((4, FRAMES, 128), BF16),
            v((4, 4, 2, 2, 32, 128), BF16),
            v((4, 2, 2, 4, 8, 128), F32),
            v((3, FRAMES, 128), BF16),
            v((7, 4, 2, 8, 128), F32),
            v((4, 2, 8, 128), F32),
            v((8, 8, 128), F32),
            v((8, 4, 2, 32, 128), BF16),
            v((4, 2, 32, 128), F32),
            v((3, 2, 32, 128), F32),
            v((2, 4, 8, 128), F32),
            v((7, 8, 128), F32),
            v((8, 256), F32),
            v((16, 8, 256), F32),
            v((16, 5, 128), F32),
            v((15, 5, 128), F32),
            v((32, 5, 128), F32),
            v((16, 5, 128), F32),
            pltpu.SemaphoreType.DMA((4,)),
            pltpu.SemaphoreType.DMA((25,)),
            pltpu.SemaphoreType.DMA((25,)),
        ],
        compiler_params=pltpu.CompilerParams(
            collective_id=1, has_side_effects=True, vmem_limit_bytes=48 << 20
        ),
    )(gated, cotangent, lengths, taps, gain.reshape(1, D), weight)
    return rows, dweight, dkernel, dgain.reshape(D)


def solution(mesh):
    return jax.shard_map(
        body,
        mesh=mesh,
        in_specs=(
            P("dp", "seq", None),
            P("dp", "seq", None),
            P("dp", None),
            P(),
            P(),
            P("seq", None),
        ),
        out_specs=(P("dp", "seq", None), P("seq", None), P(), P()),
        check_vma=False,
    )
```

time: 430 us -> 78.9 us (0.18); the launches traced: 425 us -> 78.6 us
  waiting for transfers between devices: 260 us -> 0 us
  blocking collectives: 106 us -> 0 us
  Pallas kernels: 0 us -> 69.6 us
  other arithmetic: 24.7 us -> 0 us
  between operations: 13.9 us -> 0.66 us
  matrix products: 8.07 us -> 0 us
  starting transfers between devices: 7.47 us -> 0 us
    psum x1 -> x0, waiting for transfers between devices: 145 us -> none  [body(): grad_weight = lax.psum(partial_value, 'dp')]
    psum x1 -> x0, blocking collectives: 106 us -> none  [body(): grad_kernel, grad_gain = lax.psum((kernel_terms, gain_terms), ('dp', 'seq'))]
    all_gather x1 -> x0, waiting for transfers between devices: 76.9 us -> none  [body(): lax.all_gather(out_weight, 'seq', axis=0, tiled=True)]
    pallas_call x0 -> x1, Pallas kernels: none -> 69.6 us  [body(): pl.pallas_call(kernel, out_shape=(jax.ShapeDtypeStruct((1, FRAMES, D), BF...]
    reduce_scatter x1 -> x0, waiting for transfers between devices: 31.5 us -> none  [body(): lax.psum_scatter(lax.dot_general(act, upstream, (((0,), (0,)), ((), ())),...]
    broadcast_in_dim x1 -> x0, other arithmetic: 13.4 us -> none  [body(): grad_rows.astype(jnp.bfloat16)[None]]
    reduce_sum x4 -> x0, other arithmetic: 8.85 us -> none  [the longest x1 4.51 us: tap_products(): jnp.sum(grads * values[lead_row:lead_row + row_count] * inside, axis=0)]
    dot_general x2 -> x0, matrix products: 8.07 us -> none  [the longest x1 4.58 us: body(): lax.dot_general(upstream, lax.all_gather(out_weight, 'seq', axis=0, tiled...]
  transfers between devices with their start and end apart: 7 -> 0, of which waited for: 4 -> 0; matrix products, arithmetic and copies ran while one was open for 8% -> 0% of each run, Pallas kernels for 0% -> 0%
where the time goes in v1:
time: 78.9 us; the launch traced here: 78.6 us
  Pallas kernels  69.6 us (88%)
  local copies, waits for them, and re-layouts  8.31 us (11%)
    pallas_call x1, Pallas kernels, body(): pl.pallas_call(kernel, out_shape=(jax.ShapeDtypeStruct((1, FRAMES, D), BF...  69.6 us
    unnamed x16, local copies, waits for them, and re-layouts  8.31 us

profile of v1, /device:TPU:6, one launch (start us, length us, event | category | flops | bytes accessed | tf_op | source)
XLA Modules:
  0.0 78.6 jit_solution(985900081498486107)
XLA Ops:
  0.6 0.0 copy-start.5
  0.6 0.6 copy-done.5
  1.3 0.0 copy-start
  1.3 1.2 %copy-done = bf16[1,512,1024]{2,1,0:T(8,128)(2,1)S(1)} copy-done((bf16[1,512,1024]{2,1,0:T(8,128)(2,1)S(1)}, bf16[1,512,1024]{2,1,0:T(8,128)(2,1)}, u32[]{:S(2)}) %copy-start) | copy-done | bytes 1048600
  2.5 0.0 copy-start.1
  2.5 1.2 %copy-done.1 = bf16[1,512,1024]{2,1,0:T(8,128)(2,1)S(1)} copy-done((bf16[1,512,1024]{2,1,0:T(8,128)(2,1)S(1)}, bf16[1,512,1024]{2,1,0:T(8,128)(2,1)}, u32[]{:S(2)}) %copy-start.1) | copy-done | bytes 1048600
  3.7 0.0 copy-start.2
  3.7 0.8 %copy-done.2 = f32[9,1024]{1,0:T(8,128)S(1)} copy-done((f32[9,1024]{1,0:T(8,128)S(1)}, f32[9,1024]{1,0:T(8,128)}, u32[]{:S(2)}) %copy-start.2) | copy-done | bytes 36888
  4.6 0.0 copy-start.3
  4.6 0.8 %copy-done.3 = bf16[32,1024]{1,0:T(8,128)(2,1)S(1)} copy-done((bf16[32,1024]{1,0:T(8,128)(2,1)S(1)}, bf16[32,1024]{1,0:T(8,128)(2,1)}, u32[]{:S(2)}) %copy-start.3) | copy-done | bytes 65560
  5.4 0.0 copy-start.4
  5.4 0.7 copy-done.4
  6.1 69.6 %shard_map.93 = (bf16[1,512,1024]{2,1,0:T(8,128)(2,1)S(1)}, f32[32,1024]{1,0:T(8,128)S(1)}, f32[9,1024]{1,0:T(8,128)S(1)}, f32[1,1024]{1,0:T(1,128)S(1)}) custom-call(bf16[1,512,1024]{2,1,0:T(8,128)(2,1)S(1)} %copy-done, bf16[1,512,1024]{2,1,0:T(8,128)(2,1)S(1)} %copy-done.1, s32[1,8]{1,0:T(1,128)S(1)} %copy-done.5, f32[9,1024]{1,0:T(8,128)S(1)} %copy-done.2, ...), custom_call_target="tpu_custom_call" | custom-call | tf_op jit(solution)/shard_map/pallas_call | solution.py:456
  75.7 1.0 %copy.14 = bf16[1,512,1024]{2,1,0:T(8,128)(2,1)} copy(bf16[1,512,1024]{2,1,0:T(8,128)(2,1)S(1)} %get-tuple-element.16) | data formatting | bytes 2097152
  76.7 0.7 copy.15
  77.3 0.6 copy.16
  78.0 0.6 copy.17
Async XLA Ops:
  0.6 0.7 copy-start.5
  1.3 1.2 %copy-start = (bf16[1,512,1024]{2,1,0:T(8,128)(2,1)S(1)}, bf16[1,512,1024]{2,1,0:T(8,128)(2,1)}, u32[]{:S(2)}) copy-start(bf16[1,512,1024]{2,1,0:T(8,128)(2,1)} %gated.1) | copy-start | bytes 3145732
  2.5 1.2 %copy-start.1 = (bf16[1,512,1024]{2,1,0:T(8,128)(2,1)S(1)}, bf16[1,512,1024]{2,1,0:T(8,128)(2,1)}, u32[]{:S(2)}) copy-start(bf16[1,512,1024]{2,1,0:T(8,128)(2,1)} %cot_hbm.1) | copy-start | bytes 3145732
  3.7 0.8 %copy-start.2 = (f32[9,1024]{1,0:T(8,128)S(1)}, f32[9,1024]{1,0:T(8,128)}, u32[]{:S(2)}) copy-start(f32[9,1024]{1,0:T(8,128)} %taps.1) | copy-start | bytes 110596
  4.6 0.8 %copy-start.3 = (bf16[32,1024]{1,0:T(8,128)(2,1)S(1)}, bf16[32,1024]{1,0:T(8,128)(2,1)}, u32[]{:S(2)}) copy-start(bf16[32,1024]{1,0:T(8,128)(2,1)} %weight.1) | copy-start | bytes 196612
  5.4 0.7 copy-start.4

commit v2 on v1

--- a/solution.py
+++ b/solution.py
@@ -23,61 +23,57 @@
 
 
 def device(x, y, z, c):
-    return (lax.rem(y, 4) * 4 + x, z * 4 + lax.div(y, 4) * 2 + c)
+    return ((y & 3) * 4 + x, z * 4 + (y >> 2) * 2 + c)
 
 
 def kernel(
-    gated, cot_hbm, lengths, taps, gain, weight,
+    gated, cot_hbm, lengths_hbm, taps_hbm, gain_hbm, weight,
     out_rows, out_weight, out_kernel, out_gain,
-    xb, cot, cot_far, halo, xw, ids, mask, kb, normed, sig, inv, act, act_far, wfull,
+    xb, cot, cot_far, halo, relay, xw, ids, mask, kb, normed, sig, inv, act, act_far, wfull,
     back, bcw, tacc,
     ga, gd, sa1, ra1, ra2, sa2, ra3, rd1, sd1, rd2, sd2, rd3, final, gathered,
-    kp, rk1, rk2, kfull,
+    kp, rk1, rk2, kfull, lengths, taps, gain, rows,
     local, sends, recvs,
 ):
     dp, seq = lax.axis_index("dp"), lax.axis_index("seq")
-    yl, x = lax.div(dp, 4), lax.rem(dp, 4)
-    z, yh, c = lax.div(seq, 4), lax.rem(lax.div(seq, 2), 2), lax.rem(seq, 2)
+    yl, x = dp >> 2, dp & 3
+    z, yh, c = seq >> 2, (seq >> 1) & 1, seq & 1
     y = yh * 4 + yl
-    zy = z * 2 + yh
     flip = 1 - c
     other_core = (dp, seq + 1 - 2 * c)
-    before = (dp, lax.rem(seq + 31, 32))
-    after = (dp, lax.rem(seq + 1, 32))
-    mine = lax.div(z, 4) == c
+    before = (dp, ((seq + 31) & 31))
+    after = (dp, ((seq + 1) & 31))
+    mine = (z >> 2) == c
 
     barrier = pltpu.get_barrier_semaphore()
 
     def greet(target):
         pl.semaphore_signal(barrier, inc=1, device_id=target, device_id_type=MESH)
 
-    def column(i):
-        at = lax.rem(2 * z + c + i, 16)
-        return at, device(x, y, lax.div(at, 2), lax.rem(at, 2))
-
     def row(i):
-        at = lax.rem(2 * y + c + i, 16)
-        return at, device(x, lax.div(at, 2), z, lax.rem(at, 2))
+        at = (2 * y + c + i) & 15
+        return at, device(x, at >> 1, z, at & 1)
 
     def plane(i):
-        at = lax.rem(x * 8 + z + i, 32)
-        return device(lax.div(at, 8), y, lax.rem(at, 8), c)
-
-    def slabs(i):
-        at = lax.rem(zy + i, 16)
-        return device(x, lax.rem(at, 2) * 4 + yl, lax.div(at, 2), c)
+        at = (x * 8 + z + i) & 31
+        return device(at >> 3, y, at & 7, c)
 
     def streams(i):
-        at = lax.rem(dp + i, 16)
+        at = (dp + i) & 15
         return (at, seq)
 
     def across_x(i):
-        at = lax.rem(x + i, 4)
+        at = (x + i) & 3
         return at, device(at, y, z, c)
 
     def across_y(i):
-        at = lax.rem(y + i, 8)
+        at = (y + i) & 7
         return at, device(x, at, z, c)
+
+    def across_z(i):
+        return device(x, y, ((z + i) & 7), c)
+
+    mirror = device(x, 7 - y, z, c)
 
     def loop(low, high, step):
         def one(i, none):
@@ -86,13 +82,12 @@
 
         lax.fori_loop(low, high, one, 0)
 
-    loop(1, 16, lambda i: greet(column(i)[1]))
-    loop(1, 16, lambda i: greet(row(i)[1]))
-    loop(1, 32, lambda i: greet(plane(i)))
-    loop(1, 16, lambda i: greet(slabs(i)))
-    loop(1, 16, lambda i: greet(streams(i)))
-    greet(before)
-    greet(after)
+    for i in (4, 3, 5, 2, 6, 1, 7):
+        greet(across_z(i))
+        greet(across_y(i)[1])
+    for i in (2, 1, 3):
+        greet(across_x(i)[1])
+    greet(other_core)
 
     def copy(group, source, target_ref, target):
         return pltpu.make_async_remote_copy(
@@ -101,28 +96,124 @@
         )
 
     def send(group, source, target_ref, target):
+        started.add(group)
+        pending.add(group)
         copy(group, source, target_ref, target).start()
 
-    def arrived(group, ref):
-        copy(group, ref, ref, other_core).wait_recv()
-
-    def sent(group, ref):
-        copy(group, ref, ref, other_core).wait_send()
-
-    (HALO_A, HALO_B, W_THIN, W_WIDE, W_X, W_C1, W_C2, COT, ACT, RA1, RA2, RA3, RD1, RD2, RD3,
-     GATHER, K1, K2, K3, BACK_A, BACK_B) = range(21)
-    ACTS = 21
+    def arrived(group):
+        whole = size_of[group]
+        if group in SPLIT:
+            owned(group, whole, "wait_recv")
+        else:
+            copy(group, whole, whole, other_core).wait_recv()
+        pending.discard(group)
+
+    def sent(group):
+        whole = size_of[group]
+        if group == RELAY:
+            pl.when(crossing)(lambda: copy(group, whole, whole, other_core).wait_send())
+        elif group in SPLIT:
+            owned(group, whole, "wait_send")
+        else:
+            copy(group, whole, whole, other_core).wait_send()
+
+    def owned(group, whole, wait):
+        @pl.when(mine)
+        def _():
+            part = whole.at[pl.ds(0, 7)]
+            getattr(copy(group, part, part, other_core), wait)()
+
+        @pl.when(jnp.logical_not(mine))
+        def _():
+            getattr(copy(group, whole, whole, other_core), wait)()
+
+    (HALO_NEAR, HALO_FAR, RELAY, W_MIRROR, W_Z1, W_Z2, W_Z3, W_S1, W_S2, W_XOWN, W_XSIB, W_Y, W_C1, W_C2, W_C3,
+     COT, RA1, RA2, RA3, RD1, RD2, RD3, GATHER, K1, K2, K3, BACK_A, BACK_B) = range(28)
+    ACTS = 28
+    SPLIT = (RA3, RD1)
+    started, pending = set(), set()
+    seven = wfull.at[pl.ds(0, 7), 0, 0]
+    size_of = {
+        HALO_NEAR: halo.at[0], HALO_FAR: halo.at[0], RELAY: relay,
+        W_MIRROR: wfull.at[0, 0, 0, :, pl.ds(0, 384)],
+        W_Z1: seven.at[:, :, pl.ds(0, 128)], W_S1: seven.at[:, :, pl.ds(0, 128)],
+        W_Z2: seven.at[:, :, pl.ds(0, 256)], W_S2: seven.at[:, :, pl.ds(0, 256)],
+        W_Z3: seven.at[:, pl.ds(0, 16), pl.ds(0, 128)],
+        W_XOWN: wfull.at[:, 0, 0, :, pl.ds(0, 384)], W_XSIB: wfull.at[:, 0, 0, :, pl.ds(0, 384)],
+        W_Y: wfull.at[:, 0, 0, pl.ds(0, 16), pl.ds(0, 896)],
+        W_C1: wfull.at[:, 0, 0, :, pl.ds(0, 512)], W_C2: wfull.at[:, 0, 0, :, pl.ds(0, 512)],
+        W_C3: wfull.at[:, 0, :, :, pl.ds(0, 512)],
+        COT: cot_far,
+        RA1: ra1, RA2: ra2, RA3: ra3, RD1: rd1, RD2: rd2, RD3: rd3,
+        GATHER: gathered.at[pl.ds(0, 15)],
+        K1: rk1, K2: rk2.at[pl.ds(0, 31)], K3: kfull.at[pl.ds(0, 15)],
+        BACK_A: bcw.at[:, pl.ds(0, 8)], BACK_B: bcw.at[:, pl.ds(0, 8)],
+    }
+    for q in range(4):
+        size_of[ACTS + q] = act_far.at[pl.ds(128 * q, 128)]
 
     get_x = pltpu.make_async_copy(gated.at[0], xb, local.at[0])
     thin = pl.ds(pl.multiple_of(128 * x, 128), 128)
-    wide = pl.ds(512, 512)
-    get_thin = pltpu.make_async_copy(weight.at[:, thin], wfull.at[zy, c, :, thin], local.at[1])
-    get_wide = pltpu.make_async_copy(weight.at[:, wide], wfull.at[zy, c, :, wide], local.at[3])
+    direct = pl.ds(512, 256)
+    corner = (
+        pl.ds(pl.multiple_of(16 * (yl >> 1), 16), 16),
+        pl.ds(pl.multiple_of(768 + 128 * (yl & 1), 128), 128),
+    )
+    get_w = [
+        pltpu.make_async_copy(weight.at[:, thin], wfull.at[z, yh, c, :, thin], local.at[1]),
+        pltpu.make_async_copy(weight.at[:, direct], wfull.at[z, yh, c, :, direct], local.at[3]),
+        pltpu.make_async_copy(weight.at[corner], wfull.at[(z, yh, c) + corner], local.at[7]),
+    ]
     get_cot = pltpu.make_async_copy(cot_hbm.at[0], cot, local.at[2])
-    get_x.start()
-    get_thin.start()
-    get_wide.start()
-    get_cot.start()
+    small = [
+        pltpu.make_async_copy(source, target, local.at[4 + i])
+        for i, (source, target) in enumerate(
+            ((lengths_hbm, lengths), (taps_hbm, taps), (gain_hbm, gain))
+        )
+    ]
+    for get in get_w + [get_x] + small + [get_cot]:
+        get.start()
+
+    for get in get_w:
+        get.wait()
+    pl.semaphore_wait(barrier, 1 + 3 + 7 + 7)
+
+    def same(group, part, target):
+        send(group, part, part, target)
+
+    own_thin, own_direct = wfull.at[z, yh, c, :, thin], wfull.at[z, yh, c, :, direct]
+    own_corner = wfull.at[(z, yh, c) + corner]
+    same(W_MIRROR, own_thin, mirror)
+    same(W_MIRROR, own_direct, mirror)
+    for i in (4, 3, 5, 2, 6, 1, 7):
+        same(W_Z1, own_thin, across_z(i))
+    get_x.wait()
+    last, first = xb.at[pl.ds(FRAMES - 16, 16)], xb.at[pl.ds(0, 16)]
+    crossing = yh == c
+    opposite = device(x, (y + 4) & 7, z, 1 - c)
+
+    @pl.when(c == 1)
+    def _():
+        send(HALO_NEAR, first, halo.at[1], other_core)
+
+    @pl.when(c == 0)
+    def _():
+        send(HALO_NEAR, last, halo.at[0], other_core)
+
+    @pl.when(jnp.logical_and(crossing, c == 1))
+    def _():
+        send(RELAY, last, relay, across_z(1))
+
+    @pl.when(jnp.logical_and(crossing, c == 0))
+    def _():
+        send(RELAY, first, relay, across_z(7))
+
+    loop(1, 8, lambda i: same(W_Z3, own_corner, across_z(i)))
+    loop(1, 8, lambda i: same(W_Z2, own_direct, across_z(i)))
+    get_cot.wait()
+    send(COT, cot, cot_far, other_core)
+    for get in small:
+        get.wait()
 
     start = seq * FRAMES
     pos = lax.broadcasted_iota(jnp.int32, (FRAMES + 16, 128), 0) + (start - 8)
@@ -143,24 +234,6 @@
             mask[k, pl.ds(r, 32), :] = jnp.where(ids[pl.ds(r + 4 + k, 32), :] == own, 1.0, 0.0)
 
     loop(0, FRAMES // 32, masks)
-    get_thin.wait()
-    get_wide.wait()
-    get_x.wait()
-    pl.semaphore_wait(barrier, 15 + 15 + 31 + 15 + 15 + 2)
-
-    send(HALO_A, xb.at[pl.ds(FRAMES - 16, 16)], halo.at[0], after)
-    send(HALO_B, xb.at[pl.ds(0, 16)], halo.at[1], before)
-
-    def send_thin(i):
-        send(W_THIN, wfull.at[zy, c, :, thin], wfull.at[zy, c, :, thin], slabs(i))
-
-    def send_wide(i):
-        send(W_WIDE, wfull.at[zy, c, :, wide], wfull.at[zy, c, :, wide], slabs(i))
-
-    loop(1, 16, send_thin)
-    loop(1, 16, send_wide)
-    get_cot.wait()
-    send(COT, cot, cot_far, other_core)
 
     def widen(i):
         r = pl.multiple_of(i * 32, 32)
@@ -169,12 +242,6 @@
             xw[j, pl.ds(r + 8, 32), :] = value[:, LANES[j]]
 
     loop(0, FRAMES // 32, widen)
-    arrived(HALO_A, halo.at[0])
-    arrived(HALO_B, halo.at[1])
-    low, high = halo[0].astype(F32), halo[1].astype(F32)
-    for j in range(8):
-        xw[j, 0:8, :] = low[8:16, LANES[j]]
-        xw[j, FRAMES + 8 : FRAMES + 16, :] = high[0:8, LANES[j]]
 
     def spread(value):
         return jnp.tile(value, (ROWS // 8, 1))
@@ -208,18 +275,61 @@
             sig[pl.ds(r, ROWS), LANES[j]] = logistic
             act[j // 4, pl.ds(r, ROWS), LANES[j % 4]] = (scaled * logistic).astype(BF16)
 
-    for q in range(4):
-        loop(q * 4, q * 4 + 4, forward)
+    def send_act(q):
         block = pl.ds(128 * q, 128)
         send(ACTS + q, act.at[flip, block], act_far.at[block], other_core)
-        if q == 2:
-            arrived(W_THIN, wfull.at[pl.ds(0, 15), c, :, pl.ds(0, 128)])
-            for i in (1, 3, 2):
-                send(W_X, wfull.at[:, c, :, thin], wfull.at[:, c, :, thin], across_x(i)[1])
-
-    arrived(COT, cot_far)
+
+    loop(4, 8, forward)
+    send_act(1)
+    arrived(COT)
+
+    @pl.when(crossing)
+    def _():
+        arrived(RELAY)
+
+        @pl.when(c == 1)
+        def _():
+            send(HALO_FAR, relay, halo.at[0], opposite)
+
+        @pl.when(c == 0)
+        def _():
+            send(HALO_FAR, relay, halo.at[1], opposite)
+
+    @pl.when(jnp.logical_and(jnp.logical_not(crossing), c == 1))
+    def _():
+        send(HALO_FAR, last, halo.at[0], opposite)
+
+    @pl.when(jnp.logical_and(jnp.logical_not(crossing), c == 0))
+    def _():
+        send(HALO_FAR, first, halo.at[1], opposite)
+
+    loop(8, 12, forward)
+    send_act(2)
+    arrived(W_MIRROR)
+    sib_thin, sib_direct = wfull.at[z, 1 - yh, c, :, thin], wfull.at[z, 1 - yh, c, :, direct]
+    loop(1, 8, lambda i: same(W_S1, sib_thin, across_z(i)))
+    loop(1, 8, lambda i: same(W_S2, sib_direct, across_z(i)))
+    loop(1, 4, forward)
+    arrived(W_Z1)
+    for i in (1, 3, 2):
+        same(W_XOWN, wfull.at[:, yh, c, :, thin], across_x(i)[1])
+    arrived(W_Z3)
+    own_corners = wfull.at[(slice(None), yh, c) + corner]
+    loop(1, 8, lambda i: same(W_Y, own_corners, across_y(i)[1]))
+    loop(12, 15, forward)
+    arrived(HALO_NEAR)
+    arrived(HALO_FAR)
+    low, high = halo[0].astype(F32), halo[1].astype(F32)
+    for j in range(8):
+        xw[j, 0:8, :] = low[8:16, LANES[j]]
+        xw[j, FRAMES + 8 : FRAMES + 16, :] = high[0:8, LANES[j]]
+    forward(0)
+    send_act(0)
+    forward(15)
+    send_act(3)
+
     for q in range(4):
-        arrived(ACTS + q, act_far.at[pl.ds(128 * q, 128)])
+        arrived(ACTS + q)
     over_frames = (((0,), (0,)), ((), ()))
     for i in (1, 3, 2, 0):
         at, target = across_x(i)
@@ -234,10 +344,13 @@
             sa1[...] = value[:, :128].reshape(4, 2, 2, 4, 8, 128)
         else:
             ga[at] = value[:, :128].astype(BF16)
-            send(RA1, ga.at[at], ra1.at[i - 1], target)
+        if i == 3:
+            arrived(W_S1)
+            for k in (1, 3, 2):
+                same(W_XSIB, wfull.at[:, 1 - yh, c, :, thin], across_x(k)[1])
 
     def owner(t):
-        zi, ci = lax.div(t, 2), lax.rem(t, 2)
+        zi, ci = t >> 1, t & 1
         zt = 4 * c + zi
         return zi, ci, jnp.logical_and(zt == z, ci == c), device(x, y, zt, ci)
 
@@ -252,17 +365,26 @@
         def _():
             send(RD1, gd.at[:, zi, :, ci], rd1.at[z], target)
 
+    for i in (1, 3, 2):
+        at, target = across_x(i)
+        send(RA1, ga.at[at], ra1.at[i - 1], target)
     loop(0, 8, send_d1)
 
-    arrived(W_WIDE, wfull.at[pl.ds(0, 15), c, :, wide])
-    send(W_C1, wfull.at[:, c, :, wide], wfull.at[:, c, :, wide], other_core)
-    arrived(W_X, wfull.at[pl.ds(0, 12), c, :, wide])
-    send(W_C2, wfull.at[:, c, :, pl.ds(0, 512)], wfull.at[:, c, :, pl.ds(0, 512)], other_core)
-    arrived(W_C1, wfull.at[:, flip, :, wide])
-    arrived(W_C2, wfull.at[:, flip, :, pl.ds(0, 512)])
+    first_half, second_half = pl.ds(0, 512), pl.ds(512, 512)
+    arrived(W_XOWN)
+    same(W_C1, wfull.at[:, yh, c, :, first_half], other_core)
+    arrived(W_Z2)
+    arrived(W_S2)
+    arrived(W_Y)
+    same(W_C3, wfull.at[:, :, c, :, second_half], other_core)
+    arrived(W_XSIB)
+    same(W_C2, wfull.at[:, 1 - yh, c, :, first_half], other_core)
+    arrived(W_C3)
+    arrived(W_C1)
+    arrived(W_C2)
 
     def matmul(i):
-        value = wfull[pl.ds(4 * i, 4)].reshape(256, D)
+        value = wfull[pl.ds(2 * i, 2)].reshape(256, D)
         back[:, pl.ds(pl.multiple_of(256 * i, 256), 256)] = lax.dot_general(
             cot[...], value, (((1,), (1,)), ((), ())), preferred_element_type=F32
         )
@@ -325,7 +447,7 @@
 
     loop(1, 16, send_k1)
 
-    arrived(RA1, ra1)
+    arrived(RA1)
     total = sa1[...].reshape(FRAMES, 128)
     sa1[...] = (
         total + ra1[0].astype(F32) + ra1[1].astype(F32) + ra1[2].astype(F32)
@@ -333,42 +455,39 @@
 
     def send_a2(i):
         at, target = across_y(i)
-        send(RA2, sa1.at[:, lax.div(at, 4), :, lax.rem(at, 4)], ra2.at[i - 1], target)
+        send(RA2, sa1.at[:, at >> 2, :, at & 3], ra2.at[i - 1], target)
 
     loop(1, 8, send_a2)
 
-    def owned(group, ref):
-        @pl.when(mine)
-        def _():
-            arrived(group, ref.at[pl.ds(0, 7)])
-
-        @pl.when(jnp.logical_not(mine))
-        def _():
-            arrived(group, ref)
-
-    owned(RD1, rd1)
+    arrived(RD1)
     sd1[...] = add_up([rd1[i].astype(F32) for i in range(8)])
     for i in (1, 3, 2):
         at, target = across_x(i)
         send(RD2, sd1.at[at], rd2.at[i - 1], target)
 
-    arrived(K1, rk1)
+    arrived(K1)
     me = x * 8 + z
     rk2[me] = add_up([kp[2 * y + c]] + [rk1[i] for i in range(15)])
     loop(1, 32, lambda i: send(K2, rk2.at[me], rk2.at[me], plane(i)))
 
-    arrived(BACK_A, bcw.at[:, pl.ds(0, 8)])
-    arrived(BACK_B, bcw.at[:, pl.ds(FRAMES + 8, 8)])
+    arrived(BACK_A)
+    arrived(BACK_B)
+
+    put_rows = [
+        pltpu.make_async_copy(rows.at[half], out_rows.at[0, half], local.at[8 + i])
+        for i, half in enumerate((pl.ds(0, 256), pl.ds(256, 256)))
+    ]
 
     def rows_out(i):
         r = pl.multiple_of(i * ROWS, ROWS)
         parts = conv(bcw, r, True)
         for j in range(8):
-            out_rows[0, pl.ds(r, ROWS), LANES[j]] = parts[j].astype(BF16)
+            rows[pl.ds(r, ROWS), LANES[j]] = parts[j].astype(BF16)
 
     loop(0, 8, rows_out)
-
-    arrived(RA2, ra2)
+    put_rows[0].start()
+
+    arrived(RA2)
     sa2[...] = add_up([sa1[:, yh, :, yl]] + [ra2[i] for i in range(7)])
 
     def send_a3(t):
@@ -384,70 +503,60 @@
 
     loop(0, 8, send_a3)
 
-    arrived(RD2, rd2)
+    arrived(RD2)
     sd2[...] = add_up([sd1[x], rd2[0], rd2[1], rd2[2]]).reshape(2, 4, 8, 128)
 
     def send_d3(i):
         at, target = across_y(i)
-        send(RD3, sd2.at[lax.div(at, 4), lax.rem(at, 4)], rd3.at[i - 1], target)
+        send(RD3, sd2.at[at >> 2, at & 3], rd3.at[i - 1], target)
 
     loop(1, 8, send_d3)
 
     loop(8, 16, rows_out)
-
-    arrived(K2, rk2.at[pl.ds(0, 31)])
+    put_rows[1].start()
+
+    arrived(K2)
     own = 2 * y + c
     kfull[own] = add_up([rk2[i] for i in range(32)])
     loop(1, 16, lambda i: send(K3, kfull.at[own], kfull.at[own], row(i)[1]))
 
-    owned(RA3, ra3)
+    arrived(RA3)
     final[:, 0:128] = add_up([ra3[i] for i in range(8)])
-    arrived(RD3, rd3)
+    arrived(RD3)
     final[:, 128:256] = add_up([sd2[yh, yl]] + [rd3[i] for i in range(7)])
     gathered[dp] = final[...]
     loop(1, 16, lambda i: send(GATHER, final, gathered.at[dp], streams(i)))
 
-    arrived(K3, kfull.at[pl.ds(0, 15)])
+    arrived(K3)
     for j in range(8):
         out_kernel[0:5, LANES[j]] = kfull[2 * j]
         out_kernel[5:9, LANES[j]] = kfull[2 * j + 1, 0:4]
         out_gain[0:1, LANES[j]] = kfull[2 * j + 1, 4:5]
-    arrived(GATHER, gathered.at[pl.ds(0, 15)])
+    arrived(GATHER)
     for a in range(4):
         for b in range(4):
             out_weight[8 * a : 8 * a + 8, 256 * b : 256 * b + 256] = gathered[4 * a + b]
 
-    sent(HALO_A, halo.at[0])
-    sent(HALO_B, halo.at[1])
-    sent(W_THIN, wfull.at[pl.ds(0, 15), c, :, pl.ds(0, 128)])
-    sent(W_WIDE, wfull.at[pl.ds(0, 15), c, :, wide])
-    sent(W_X, wfull.at[pl.ds(0, 12), c, :, wide])
-    sent(W_C1, wfull.at[:, c, :, wide])
-    sent(W_C2, wfull.at[:, c, :, wide])
-    sent(COT, cot)
-    for q in range(4):
-        sent(ACTS + q, act_far.at[pl.ds(128 * q, 128)])
-    sent(RA1, ra1)
-    sent(RA2, ra2)
-
-    @pl.when(mine)
-    def _():
-        sent(RA3, ra3.at[pl.ds(0, 7)])
-        sent(RD1, rd1.at[pl.ds(0, 7)])
-
-    @pl.when(jnp.logical_not(mine))
-    def _():
-        sent(RA3, ra3)
-        sent(RD1, rd1)
-
-    sent(RD2, rd2)
-    sent(RD3, rd3)
-    sent(GATHER, gathered.at[pl.ds(0, 15)])
-    sent(K1, rk1)
-    sent(K2, rk2.at[pl.ds(0, 31)])
-    sent(K3, kfull.at[pl.ds(0, 15)])
-    sent(BACK_A, bcw.at[:, pl.ds(0, 8)])
-    sent(BACK_B, bcw.at[:, pl.ds(0, 8)])
+    put_rows[0].wait()
+    put_rows[1].wait()
+    for group in sorted(started):
+        sent(group)
+
+
+def hand_over(*refs):
+    source, target, held, sems = refs[0:4], refs[4:8], refs[8:12], refs[12]
+    parts = [(0, (0, pl.ds(128 * q, 128))) for q in range(4)] + [(i, ...) for i in (1, 2, 3)]
+    into, out = [], []
+    for i, (k, at) in enumerate(parts):
+        into.append(pltpu.make_async_copy(source[k].at[at], held[k].at[at], sems.at[0, i]))
+        out.append(pltpu.make_async_copy(held[k].at[at], target[k].at[at], sems.at[1, i]))
+    for one in into:
+        one.start()
+    for first, second in zip(into, out):
+        first.wait()
+        second.start()
+    for one in out:
+        one.wait()
 
 
 def body(gated, cotangent, lengths, taps, gain, weight):
@@ -461,13 +570,14 @@
             jax.ShapeDtypeStruct((KW, D), F32),
             jax.ShapeDtypeStruct((1, D), F32),
         ),
-        in_specs=[hbm, hbm, pl.BlockSpec(memory_space=pltpu.SMEM), vmem, vmem, hbm],
-        out_specs=(vmem, vmem, vmem, vmem),
+        in_specs=[hbm] * 6,
+        out_specs=(hbm, vmem, vmem, vmem),
         scratch_shapes=[
             v((FRAMES, D), BF16),
             v((FRAMES, D), BF16),
             v((FRAMES, D), BF16),
             v((2, 16, D), BF16),
+            v((16, D), BF16),
             v((8, FRAMES + 16, 128), F32),
             v((FRAMES + 16, 128), jnp.int32),
             v((KW, FRAMES, 128), F32),
@@ -477,7 +587,7 @@
             v((FRAMES, 128), F32),
             v((2, FRAMES, 512), BF16),
             v((FRAMES, 512), BF16),
-            v((16, 2, 32, D), BF16),
+            v((8, 2, 2, 32, D), BF16),
             v((FRAMES, D), F32),
             v((8, FRAMES + 16, 128), F32),
             v((KW, 8, D), F32),
@@ -499,14 +609,27 @@
             v((15, 5, 128), F32),
             v((32, 5, 128), F32),
             v((16, 5, 128), F32),
-            pltpu.SemaphoreType.DMA((4,)),
-            pltpu.SemaphoreType.DMA((25,)),
-            pltpu.SemaphoreType.DMA((25,)),
+            pltpu.SMEM((1, 8), jnp.int32),
+            v((KW, D), F32),
+            v((1, D), F32),
+            v((FRAMES, D), BF16),
+            pltpu.SemaphoreType.DMA((10,)),
+            pltpu.SemaphoreType.DMA((32,)),
+            pltpu.SemaphoreType.DMA((32,)),
         ],
         compiler_params=pltpu.CompilerParams(
-            collective_id=1, has_side_effects=True, vmem_limit_bytes=48 << 20
+            collective_id=1, has_side_effects=True, vmem_limit_bytes=60 << 20
         ),
     )(gated, cotangent, lengths, taps, gain.reshape(1, D), weight)
+    results = (rows, dweight, dkernel, dgain)
+    rows, dweight, dkernel, dgain = pl.pallas_call(
+        hand_over,
+        out_shape=tuple(jax.ShapeDtypeStruct(r.shape, r.dtype) for r in results),
+        in_specs=[hbm] * 4,
+        out_specs=(hbm,) * 4,
+        scratch_shapes=[v(r.shape, r.dtype) for r in results] + [pltpu.SemaphoreType.DMA((2, 7))],
+        compiler_params=pltpu.CompilerParams(vmem_limit_bytes=60 << 20),
+    )(*results)
     return rows, dweight, dkernel, dgain.reshape(D)
 
 

time: 78.9 us -> 63.9 us (0.81)
  local copies, waits for them, and re-layouts: 8.31 us -> 0 us
  Pallas kernels: 69.6 us -> 62.4 us
    pallas_call x1, Pallas kernels: 69.6 us -> 60.3 us  [body(): pl.pallas_call(kernel, out_shape=(jax.ShapeDtypeStruct((1, FRAMES, D), BF...]
    unnamed x16 -> x0, local copies, waits for them, and re-layouts: 8.31 us -> none
    pallas_call x0 -> x1, Pallas kernels: none -> 2.09 us  [body(): pl.pallas_call(hand_over, out_shape=tuple((jax.ShapeDtypeStruct(r.shape,...]
where the time goes in v2:
time: 63.9 us; the launch traced here: 63.1 us
  Pallas kernels  62.4 us (98%)
  between operations  0.64 us (1%)
    pallas_call x1, Pallas kernels, body(): pl.pallas_call(kernel, out_shape=(jax.ShapeDtypeStruct((1, FRAMES, D), BF...  60.3 us
    pallas_call x1, Pallas kernels, body(): pl.pallas_call(hand_over, out_shape=tuple((jax.ShapeDtypeStruct(r.shape,...  2.09 us

profile of v2, /device:TPU:6, one launch (start us, length us, event | category | flops | bytes accessed | tf_op | source)
XLA Modules:
  0.0 63.1 jit_solution(8205749377228139312)
XLA Ops:
  0.6 60.3 %shard_map.93 = (bf16[1,512,1024]{2,1,0:T(8,128)(2,1)}, f32[32,1024]{1,0:T(8,128)}, f32[9,1024]{1,0:T(8,128)}, f32[1,1024]{1,0:T(1,128)}) custom-call(bf16[1,512,1024]{2,1,0:T(8,128)(2,1)} %gated.1, bf16[1,512,1024]{2,1,0:T(8,128)(2,1)} %cot_hbm.1, s32[1,8]{1,0:T(1,128)} %lengths_hbm.1, f32[9,1024]{1,0:T(8,128)} %taps_hbm.1, f32[1,1024]{1,0:T(1,128)} %bitcast.2, ...), custom_call_target="tpu_custom_call" | custom-call | tf_op jit(solution)/shard_map/pallas_call | solution.py:565
  61.0 2.1 %shard_map.94 = (bf16[1,512,1024]{2,1,0:T(8,128)(2,1)}, f32[32,1024]{1,0:T(8,128)}, f32[9,1024]{1,0:T(8,128)}, f32[1,1024]{1,0:T(1,128)}) custom-call(bf16[1,512,1024]{2,1,0:T(8,128)(2,1)} %get-tuple-element.12.refs_0_, f32[32,1024]{1,0:T(8,128)} %get-tuple-element.13.refs_1_, f32[9,1024]{1,0:T(8,128)} %get-tuple-element.14.refs_2_, ...), custom_call_target="tpu_custom_call" | custom-call | tf_op jit(solution)/shard_map/pallas_call | solution.py:625

commit v3 on v2

--- a/solution.py
+++ b/solution.py
@@ -31,8 +31,8 @@
     out_rows, out_weight, out_kernel, out_gain,
     xb, cot, cot_far, halo, relay, xw, ids, mask, kb, normed, sig, inv, act, act_far, wfull,
     back, bcw, tacc,
-    ga, gd, sa1, ra1, ra2, sa2, ra3, rd1, sd1, rd2, sd2, rd3, final, gathered,
-    kp, rk1, rk2, kfull, lengths, taps, gain, rows,
+    ga, gd, sa1, sb1, ra1, ra2, sa2, ra3, rd1, sd1, rd2, sd2, rd3, final, gathered,
+    kp, rk1, rk2, kfull, lengths, taps, gain,
     local, sends, recvs,
 ):
     dp, seq = lax.axis_index("dp"), lax.axis_index("seq")
@@ -279,60 +279,69 @@
         block = pl.ds(128 * q, 128)
         send(ACTS + q, act.at[flip, block], act_far.at[block], other_core)
 
-    loop(4, 8, forward)
-    send_act(1)
-    arrived(COT)
-
-    @pl.when(crossing)
-    def _():
-        arrived(RELAY)
-
-        @pl.when(c == 1)
-        def _():
-            send(HALO_FAR, relay, halo.at[0], opposite)
-
-        @pl.when(c == 0)
-        def _():
-            send(HALO_FAR, relay, halo.at[1], opposite)
-
-    @pl.when(jnp.logical_and(jnp.logical_not(crossing), c == 1))
-    def _():
-        send(HALO_FAR, last, halo.at[0], opposite)
-
-    @pl.when(jnp.logical_and(jnp.logical_not(crossing), c == 0))
-    def _():
-        send(HALO_FAR, first, halo.at[1], opposite)
-
-    loop(8, 12, forward)
-    send_act(2)
-    arrived(W_MIRROR)
     sib_thin, sib_direct = wfull.at[z, 1 - yh, c, :, thin], wfull.at[z, 1 - yh, c, :, direct]
-    loop(1, 8, lambda i: same(W_S1, sib_thin, across_z(i)))
-    loop(1, 8, lambda i: same(W_S2, sib_direct, across_z(i)))
-    loop(1, 4, forward)
-    arrived(W_Z1)
-    for i in (1, 3, 2):
-        same(W_XOWN, wfull.at[:, yh, c, :, thin], across_x(i)[1])
-    arrived(W_Z3)
-    own_corners = wfull.at[(slice(None), yh, c) + corner]
-    loop(1, 8, lambda i: same(W_Y, own_corners, across_y(i)[1]))
-    loop(12, 15, forward)
-    arrived(HALO_NEAR)
-    arrived(HALO_FAR)
-    low, high = halo[0].astype(F32), halo[1].astype(F32)
-    for j in range(8):
-        xw[j, 0:8, :] = low[8:16, LANES[j]]
-        xw[j, FRAMES + 8 : FRAMES + 16, :] = high[0:8, LANES[j]]
-    forward(0)
-    send_act(0)
-    forward(15)
-    send_act(3)
+
+    def step(t):
+        @pl.when(t == 2)
+        def _():
+            arrived(COT)
+
+            @pl.when(crossing)
+            def _():
+                arrived(RELAY)
+
+                @pl.when(c == 1)
+                def _():
+                    send(HALO_FAR, relay, halo.at[0], opposite)
+
+                @pl.when(c == 0)
+                def _():
+                    send(HALO_FAR, relay, halo.at[1], opposite)
+
+            @pl.when(jnp.logical_and(jnp.logical_not(crossing), c == 1))
+            def _():
+                send(HALO_FAR, last, halo.at[0], opposite)
+
+            @pl.when(jnp.logical_and(jnp.logical_not(crossing), c == 0))
+            def _():
+                send(HALO_FAR, first, halo.at[1], opposite)
+
+        @pl.when(t == 4)
+        def _():
+            arrived(W_MIRROR)
+            loop(1, 8, lambda i: same(W_S1, sib_thin, across_z(i)))
+            loop(1, 8, lambda i: same(W_S2, sib_direct, across_z(i)))
+
+        @pl.when(t == 7)
+        def _():
+            arrived(W_Z1)
+            for i in (1, 3, 2):
+                same(W_XOWN, wfull.at[:, yh, c, :, thin], across_x(i)[1])
+            arrived(W_Z3)
+            own_corners = wfull.at[(slice(None), yh, c) + corner]
+            loop(1, 8, lambda i: same(W_Y, own_corners, across_y(i)[1]))
+
+        @pl.when(t == 14)
+        def _():
+            arrived(HALO_NEAR)
+            arrived(HALO_FAR)
+            low, high = halo[0].astype(F32), halo[1].astype(F32)
+            for j in range(8):
+                xw[j, 0:8, :] = low[8:16, LANES[j]]
+                xw[j, FRAMES + 8 : FRAMES + 16, :] = high[0:8, LANES[j]]
+
+        forward((t + 1) & 15)
+        for q, last_step in ((1, 6), (2, 10), (3, 14), (0, 15)):
+            pl.when(t == last_step)(functools.partial(send_act, q))
+
+    loop(0, 16, step)
 
     for q in range(4):
         arrived(ACTS + q)
     over_frames = (((0,), (0,)), ((), ()))
-    for i in (1, 3, 2, 0):
-        at, target = across_x(i)
+
+    def product(t):
+        at = (x + t + 1) & 3
         columns = pl.ds(pl.multiple_of(256 * at, 256), 256)
         value = lax.dot_general(
             act[c], cot[:, columns], over_frames, preferred_element_type=F32
@@ -340,15 +349,16 @@
             act_far[...], cot_far[:, columns], over_frames, preferred_element_type=F32
         )
         gd[at] = value[:, 128:].astype(BF16).reshape(4, 2, 2, 32, 128)
-        if i == 0:
-            sa1[...] = value[:, :128].reshape(4, 2, 2, 4, 8, 128)
-        else:
-            ga[at] = value[:, :128].astype(BF16)
-        if i == 3:
+        ga[at] = value[:, :128].astype(BF16)
+        sa1[...] = value[:, :128]
+
+        @pl.when(t == 0)
+        def _():
             arrived(W_S1)
             for k in (1, 3, 2):
                 same(W_XSIB, wfull.at[:, 1 - yh, c, :, thin], across_x(k)[1])
 
+    loop(0, 4, product)
     def owner(t):
         zi, ci = t >> 1, t & 1
         zt = 4 * c + zi
@@ -448,14 +458,14 @@
     loop(1, 16, send_k1)
 
     arrived(RA1)
-    total = sa1[...].reshape(FRAMES, 128)
-    sa1[...] = (
-        total + ra1[0].astype(F32) + ra1[1].astype(F32) + ra1[2].astype(F32)
-    ).reshape(4, 2, 2, 4, 8, 128)
+    total = add_up([sa1[...]] + [ra1[i].astype(F32) for i in range(3)])
+    total = jnp.swapaxes(total.reshape(4, 2, 2, 4, 8, 128), 2, 3).reshape(4, 2, 4, 16, 128)
+    sa1[...] = total.reshape(FRAMES, 128)
+    sb1[...] = total.astype(BF16)
 
     def send_a2(i):
         at, target = across_y(i)
-        send(RA2, sa1.at[:, at >> 2, :, at & 3], ra2.at[i - 1], target)
+        send(RA2, sb1.at[:, at >> 2, at & 3], ra2.at[i - 1], target)
 
     loop(1, 8, send_a2)
 
@@ -473,22 +483,11 @@
     arrived(BACK_A)
     arrived(BACK_B)
 
-    put_rows = [
-        pltpu.make_async_copy(rows.at[half], out_rows.at[0, half], local.at[8 + i])
-        for i, half in enumerate((pl.ds(0, 256), pl.ds(256, 256)))
-    ]
-
     def rows_out(i):
         r = pl.multiple_of(i * ROWS, ROWS)
         parts = conv(bcw, r, True)
         for j in range(8):
-            rows[pl.ds(r, ROWS), LANES[j]] = parts[j].astype(BF16)
-
-    loop(0, 8, rows_out)
-    put_rows[0].start()
-
-    arrived(RA2)
-    sa2[...] = add_up([sa1[:, yh, :, yl]] + [ra2[i] for i in range(7)])
+            out_rows[0, pl.ds(r, ROWS), LANES[j]] = parts[j].astype(BF16)
 
     def send_a3(t):
         zi, ci, here, target = owner(t)
@@ -500,20 +499,29 @@
         @pl.when(jnp.logical_not(here))
         def _():
             send(RA3, sa2.at[zi, ci], ra3.at[z], target)
-
-    loop(0, 8, send_a3)
-
-    arrived(RD2)
-    sd2[...] = add_up([sd1[x], rd2[0], rd2[1], rd2[2]]).reshape(2, 4, 8, 128)
 
     def send_d3(i):
         at, target = across_y(i)
         send(RD3, sd2.at[at >> 2, at & 3], rd3.at[i - 1], target)
 
-    loop(1, 8, send_d3)
-
-    loop(8, 16, rows_out)
-    put_rows[1].start()
+    def result(t):
+        @pl.when(t == 8)
+        def _():
+            arrived(RA2)
+            for i in range(4):
+                own_rows = pl.ds(pl.multiple_of(128 * i + 64 * yh + 16 * yl, 16), 16)
+                pieces = [sa1[own_rows, :]] + [ra2[k, i].astype(F32) for k in range(7)]
+                sa2[i] = add_up(pieces).reshape(2, 8, 128)
+
+            loop(0, 8, send_a3)
+            arrived(RD2)
+            sd2[...] = add_up([sd1[x], rd2[0], rd2[1], rd2[2]]).reshape(2, 4, 8, 128)
+
+            loop(1, 8, send_d3)
+
+        rows_out(t)
+
+    loop(0, 16, result)
 
     arrived(K2)
     own = 2 * y + c
@@ -537,41 +545,31 @@
         for b in range(4):
             out_weight[8 * a : 8 * a + 8, 256 * b : 256 * b + 256] = gathered[4 * a + b]
 
-    put_rows[0].wait()
-    put_rows[1].wait()
     for group in sorted(started):
         sent(group)
 
 
 def hand_over(*refs):
-    source, target, held, sems = refs[0:4], refs[4:8], refs[8:12], refs[12]
-    parts = [(0, (0, pl.ds(128 * q, 128))) for q in range(4)] + [(i, ...) for i in (1, 2, 3)]
-    into, out = [], []
-    for i, (k, at) in enumerate(parts):
-        into.append(pltpu.make_async_copy(source[k].at[at], held[k].at[at], sems.at[0, i]))
-        out.append(pltpu.make_async_copy(held[k].at[at], target[k].at[at], sems.at[1, i]))
-    for one in into:
+    copies = [pltpu.make_async_copy(refs[i], refs[4 + i], refs[8].at[i]) for i in range(4)]
+    for one in copies:
         one.start()
-    for first, second in zip(into, out):
-        first.wait()
-        second.start()
-    for one in out:
+    for one in copies:
         one.wait()
 
 
 def body(gated, cotangent, lengths, taps, gain, weight):
     v = pltpu.VMEM
-    vmem, hbm = pl.BlockSpec(memory_space=v), pl.BlockSpec(memory_space=pl.ANY)
+    vmem, hbm = pl.BlockSpec(memory_space=v), pl.BlockSpec(memory_space=pltpu.HBM)
     rows, dweight, dkernel, dgain = pl.pallas_call(
         kernel,
         out_shape=(
-            jax.ShapeDtypeStruct((1, FRAMES, D), BF16),
-            jax.ShapeDtypeStruct((32, D), F32),
-            jax.ShapeDtypeStruct((KW, D), F32),
-            jax.ShapeDtypeStruct((1, D), F32),
+            v((1, FRAMES, D), BF16),
+            v((32, D), F32),
+            v((KW, D), F32),
+            v((1, D), F32),
         ),
         in_specs=[hbm] * 6,
-        out_specs=(hbm, vmem, vmem, vmem),
+        out_specs=(vmem,) * 4,
         scratch_shapes=[
             v((FRAMES, D), BF16),
             v((FRAMES, D), BF16),
@@ -593,9 +591,10 @@
             v((KW, 8, D), F32),
             v((4, FRAMES, 128), BF16),
             v((4, 4, 2, 2, 32, 128), BF16),
-            v((4, 2, 2, 4, 8, 128), F32),
+            v((FRAMES, 128), F32),
+            v((4, 2, 4, 16, 128), BF16),
             v((3, FRAMES, 128), BF16),
-            v((7, 4, 2, 8, 128), F32),
+            v((7, 4, 16, 128), BF16),
             v((4, 2, 8, 128), F32),
             v((8, 8, 128), F32),
             v((8, 4, 2, 32, 128), BF16),
@@ -612,8 +611,7 @@
             pltpu.SMEM((1, 8), jnp.int32),
             v((KW, D), F32),
             v((1, D), F32),
-            v((FRAMES, D), BF16),
-            pltpu.SemaphoreType.DMA((10,)),
+            pltpu.SemaphoreType.DMA((8,)),
             pltpu.SemaphoreType.DMA((32,)),
             pltpu.SemaphoreType.DMA((32,)),
         ],
@@ -625,10 +623,10 @@
     rows, dweight, dkernel, dgain = pl.pallas_call(
         hand_over,
         out_shape=tuple(jax.ShapeDtypeStruct(r.shape, r.dtype) for r in results),
-        in_specs=[hbm] * 4,
+        in_specs=[vmem] * 4,
         out_specs=(hbm,) * 4,
-        scratch_shapes=[v(r.shape, r.dtype) for r in results] + [pltpu.SemaphoreType.DMA((2, 7))],
-        compiler_params=pltpu.CompilerParams(vmem_limit_bytes=60 << 20),
+        scratch_shapes=[pltpu.SemaphoreType.DMA((4,))],
+        compiler_params=pltpu.CompilerParams(vmem_limit_bytes=32 << 20),
     )(*results)
     return rows, dweight, dkernel, dgain.reshape(D)
 

time: 63.9 us -> 60.6 us (0.948)
  Pallas kernels: 62.4 us -> 59.5 us
    pallas_call x1, Pallas kernels: 60.3 us -> 58.4 us  [body(): pl.pallas_call(kernel, out_shape=(v((1, FRAMES, D), BF16), v((32, D), F32...]
    pallas_call x1, Pallas kernels: 2.09 us -> 1.06 us  [body(): pl.pallas_call(hand_over, out_shape=tuple((jax.ShapeDtypeStruct(r.shape,...]
where the time goes in v3:
time: 60.6 us; the launch traced here: 60.1 us
  Pallas kernels  59.5 us (98%)
  between operations  0.64 us (1%)
    pallas_call x1, Pallas kernels, body(): pl.pallas_call(kernel, out_shape=(v((1, FRAMES, D), BF16), v((32, D), F32...  58.4 us

profile of v3, /device:TPU:6, one launch (start us, length us, event | category | flops | bytes accessed | tf_op | source)
XLA Modules:
  0.0 60.1 jit_solution(3627475413702216640)
XLA Ops:
  0.6 58.4 %shard_map.93 = (bf16[1,512,1024]{2,1,0:T(8,128)(2,1)S(1)}, f32[32,1024]{1,0:T(8,128)S(1)}, f32[9,1024]{1,0:T(8,128)S(1)}, f32[1,1024]{1,0:T(1,128)S(1)}) custom-call(bf16[1,512,1024]{2,1,0:T(8,128)(2,1)} %gated.1, bf16[1,512,1024]{2,1,0:T(8,128)(2,1)} %cot_hbm.1, s32[1,8]{1,0:T(1,128)} %lengths_hbm.1, f32[9,1024]{1,0:T(8,128)} %taps_hbm.1, ...), custom_call_target="tpu_custom_call" | custom-call | tf_op jit(solution)/shard_map/pallas_call | solution.py:563
  59.1 1.1 %shard_map.94 = (bf16[1,512,1024]{2,1,0:T(8,128)(2,1)}, f32[32,1024]{1,0:T(8,128)}, f32[9,1024]{1,0:T(8,128)}, f32[1,1024]{1,0:T(1,128)}) custom-call(bf16[1,512,1024]{2,1,0:T(8,128)(2,1)S(1)} %get-tuple-element.12.refs_0_, f32[32,1024]{1,0:T(8,128)S(1)} %get-tuple-element.13.refs_1_, f32[9,1024]{1,0:T(8,128)S(1)} %get-tuple-element.14.refs_2_, ...), custom_call_target="tpu_custom_call" | custom-call | tf_op jit(solution)/shard_map/pallas_call | solution.py:623

commit v4 on v3

--- a/solution.py
+++ b/solution.py
@@ -29,7 +29,7 @@
 def kernel(
     gated, cot_hbm, lengths_hbm, taps_hbm, gain_hbm, weight,
     out_rows, out_weight, out_kernel, out_gain,
-    xb, cot, cot_far, halo, relay, xw, ids, mask, kb, normed, sig, inv, act, act_far, wfull,
+    xb, cot, cot_far, halo, relay, xw, ids, mask, kb, normed, slope, inv, act, act_far, wfull,
     back, bcw, tacc,
     ga, gd, sa1, sb1, ra1, ra2, sa2, ra3, rd1, sd1, rd2, sd2, rd3, final, gathered,
     kp, rk1, rk2, kfull, lengths, taps, gain,
@@ -272,7 +272,7 @@
             normed[pl.ds(r, ROWS), LANES[j]] = unit
             scaled = unit * spread(kb[KW, :, LANES[j]])
             logistic = jax.nn.sigmoid(scaled)
-            sig[pl.ds(r, ROWS), LANES[j]] = logistic
+            slope[pl.ds(r, ROWS), LANES[j]] = logistic * (1.0 + scaled * (1.0 - logistic))
             act[j // 4, pl.ds(r, ROWS), LANES[j % 4]] = (scaled * logistic).astype(BF16)
 
     def send_act(q):
@@ -407,9 +407,7 @@
         for j in range(8):
             g = spread(kb[KW, :, LANES[j]])
             unit = normed[pl.ds(r, ROWS), LANES[j]]
-            logistic = sig[pl.ds(r, ROWS), LANES[j]]
-            scaled = unit * g
-            value = back[pl.ds(r, ROWS), LANES[j]] * (logistic * (1.0 + scaled * (1.0 - logistic)))
+            value = back[pl.ds(r, ROWS), LANES[j]] * slope[pl.ds(r, ROWS), LANES[j]]
             totals.append(sums[j] + fold(value * unit))
             hidden = value * g
             bcw[j, pl.ds(r + 8, ROWS), :] = hidden
@@ -426,7 +424,7 @@
         return tuple(totals)
 
     sums = lax.fori_loop(
-        0, FRAMES // ROWS, backward, tuple(jnp.zeros((8, 128), F32) for _ in range(8))
+        0, FRAMES // ROWS, backward, tuple(jnp.zeros((8, 128), F32) for _ in range(8)), unroll=2
     )
     send(BACK_A, bcw.at[:, pl.ds(FRAMES, 8)], bcw.at[:, pl.ds(0, 8)], after)
     send(BACK_B, bcw.at[:, pl.ds(8, 8)], bcw.at[:, pl.ds(FRAMES + 8, 8)], before)

time: 60.6 us -> 59.6 us (0.983)
  Pallas kernels: 59.5 us -> 58.6 us
    pallas_call x1, Pallas kernels: 58.4 us -> 57.5 us  [body(): pl.pallas_call(kernel, out_shape=(v((1, FRAMES, D), BF16), v((32, D), F32...]
where the time goes in v4:
time: 59.6 us; the launch traced here: 59.2 us
  Pallas kernels  58.6 us (98%)
  between operations  0.64 us (1%)
    pallas_call x1, Pallas kernels, body(): pl.pallas_call(kernel, out_shape=(v((1, FRAMES, D), BF16), v((32, D), F32...  57.5 us

profile of v4, /device:TPU:6, one launch (start us, length us, event | category | flops | bytes accessed | tf_op | source)
XLA Modules:
  0.0 59.2 jit_solution(10967583404467335422)
XLA Ops:
  0.6 57.5 %shard_map.93 = (bf16[1,512,1024]{2,1,0:T(8,128)(2,1)S(1)}, f32[32,1024]{1,0:T(8,128)S(1)}, f32[9,1024]{1,0:T(8,128)S(1)}, f32[1,1024]{1,0:T(1,128)S(1)}) custom-call(bf16[1,512,1024]{2,1,0:T(8,128)(2,1)} %gated.1, bf16[1,512,1024]{2,1,0:T(8,128)(2,1)} %cot_hbm.1, s32[1,8]{1,0:T(1,128)} %lengths_hbm.1, f32[9,1024]{1,0:T(8,128)} %taps_hbm.1, ...), custom_call_target="tpu_custom_call" | custom-call | tf_op jit(solution)/shard_map/pallas_call | solution.py:561
  58.1 1.1 %shard_map.94 = (bf16[1,512,1024]{2,1,0:T(8,128)(2,1)}, f32[32,1024]{1,0:T(8,128)}, f32[9,1024]{1,0:T(8,128)}, f32[1,1024]{1,0:T(1,128)}) custom-call(bf16[1,512,1024]{2,1,0:T(8,128)(2,1)S(1)} %get-tuple-element.12.refs_0_, f32[32,1024]{1,0:T(8,128)S(1)} %get-tuple-element.13.refs_1_, f32[9,1024]{1,0:T(8,128)S(1)} %get-tuple-element.14.refs_2_, ...), custom_call_target="tpu_custom_call" | custom-call | tf_op jit(solution)/shard_map/pallas_call | solution.py:621
